TPU v7x, 32 devices: a whole 2x2x4 slice. The times are simulated.
32 devices in a mesh: groups: 2 (over x), section: 8 (over z, y), sub: 2 (over core).
Axes of the slice: x: 2, y: 2, z: 4, core: 2. Of those that a mesh axis runs over, the one named last changes fastest.
Arguments:
- voltages: bfloat16 [2048, 2, 65920], P(('groups', 'section', 'sub')), parts along dimension 0, may hold values from -6 to 6
- prototype: float32 [512], replicated, may hold values from 0.02 to 0.07
- beam_weights: bfloat16 [256, 2, 1024, 1024], P(('groups', 'section', 'sub')), parts along dimension 0, may hold values from -0.125 to 0.125
- input_order: int32 [1024], replicated, may hold values from 0 to 1023, each once
- beam_order: int32 [1024], replicated, may hold values from 0 to 1023, each once
- trial_delays: int32 [256, 128], replicated, may hold values from 0 to 127, as said below
Outputs:
- dedispersed: float32 [256, 2048, 128], P(None, ('groups', 'section', 'sub')), parts along dimension 1
There are 2 independent parts, one for each index of `groups`. A program takes and returns all parts, laid end to end along the dimension named above; an argument that names none is the same for every part. Nothing has to cross between parts.
Inputs may be any that keep to these rules, and one draw needn't show every extreme that they name: `input_order`: each physical input appears once. `beam_order`: each physical beam appears once. `trial_delays`: for each trial the delays do not rise with the channel index.
All inputs are finite; a program needn't handle non-finite values.
Results may differ from a plain program's by a relative error of at most 0.0043.
Values may be sent and summed in bfloat16 or wider, within the bound.
A program may use at most 256 MiB of HBM per device.

v0:
```python
import math

import jax
import jax.numpy as jnp
from jax import lax
from jax.sharding import PartitionSpec as P

CHANS = 128
INPUTS = 1024
BEAMS = 1024
TAPS = 4
DOWN = 4
SPECTRA = 512
BINS = 128


def filter_matrix(prototype):
    channel_index = jnp.arange(CHANS, dtype=jnp.int32)
    phase_step = channel_index[:, None] * channel_index[None, :] % CHANS
    angles = 2.0 * math.pi / CHANS * phase_step.astype(jnp.float32)
    cosine = jnp.tile(jnp.cos(angles), (1, TAPS)) * prototype[None, :]
    sine_part = jnp.tile(jnp.sin(angles), (1, TAPS)) * prototype[None, :]
    real_rows = jnp.concatenate([cosine, sine_part], axis=1)
    imag_rows = jnp.concatenate([-sine_part, cosine], axis=1)
    return jnp.stack([real_rows, imag_rows], axis=0).astype(jnp.bfloat16)


def channelize(block_volts, matrix):
    input_count = block_volts.shape[0]
    frames = block_volts.reshape(input_count, 2, SPECTRA + TAPS - 1, CHANS)
    windows = jnp.concatenate(
        [
            frames[:, part_index, tap_index : tap_index + SPECTRA, :]
            for part_index in range(2)
            for tap_index in range(TAPS)
        ],
        axis=2,
    )
    result = lax.dot_general(
        matrix, windows, (((2,), (2,)), ((), ())), preferred_element_type=jnp.float32
    )
    return result.astype(jnp.bfloat16)


def fold_time(series):
    shape_head = series.shape[:-1]
    return series.reshape(shape_head + (series.shape[-1] // DOWN, DOWN)).sum(axis=-1)


def shards(voltages, prototype, beam_weights, input_order, beam_order, trial_delays):
    section_count = lax.axis_size("section")
    sub_count = lax.axis_size("sub")
    owners = section_count * sub_count
    chan_dev = CHANS // owners
    beam_dev = BEAMS // owners
    input_rows = jnp.arange(INPUTS, dtype=jnp.int32)
    channel_rows = jnp.arange(CHANS, dtype=jnp.int32)
    spectra_local = channelize(voltages, filter_matrix(prototype))
    physical = jnp.take(input_order, input_rows)
    position_of = (
        jnp.zeros((INPUTS,), jnp.int32).at[physical].set(jnp.arange(INPUTS, dtype=jnp.int32))
    )
    weight_real = beam_weights[:, 0]
    weight_imag = beam_weights[:, 1]
    ordered = jnp.take(
        lax.all_to_all(spectra_local, ("section", "sub"), split_axis=1, concat_axis=2, tiled=True),
        position_of,
        axis=2,
    )
    with_real = jnp.einsum(
        "cbi,pcit->pcbt", weight_real, ordered, preferred_element_type=jnp.float32
    )
    with_imag = jnp.einsum(
        "cbi,pcit->pcbt", weight_imag, ordered, preferred_element_type=jnp.float32
    )
    beam_real = with_real[0] - with_imag[1]
    beam_imag = with_real[1] + with_imag[0]
    power = beam_real * beam_real + beam_imag * beam_imag
    power = jnp.take(power, beam_order, axis=1)
    outgoing = fold_time(power)
    outgoing = outgoing.reshape(chan_dev, owners, beam_dev, outgoing.shape[2])
    half = BINS // 2 + 1
    delay_table = jnp.transpose(jnp.take(trial_delays, channel_rows, axis=1))
    sample_index = jnp.arange(BINS, dtype=jnp.int32)
    freq_index = jnp.arange(half, dtype=jnp.int32)
    half_angles = (
        2.0
        * math.pi
        / BINS
        * (freq_index[:, None] * sample_index[None, :] % BINS).astype(jnp.float32)
    )
    forward_cos = jnp.cos(half_angles)
    forward_sin = -jnp.sin(half_angles)
    edge = (freq_index == 0) | (freq_index == BINS // 2)
    fold_weight = (jnp.where(edge, 1.0, 2.0) / BINS).astype(jnp.float32)[:, None]
    inverse_cos = fold_weight * forward_cos
    inverse_sin = fold_weight * forward_sin
    twiddle_angles = (
        2.0
        * math.pi
        / BINS
        * (sample_index[:, None] * freq_index[None, :] % BINS).astype(jnp.float32)
    )
    twiddle = jnp.concatenate([jnp.cos(twiddle_angles), jnp.sin(twiddle_angles)], axis=1)
    twiddle_high = twiddle.astype(jnp.bfloat16)
    twiddle_low = (twiddle - twiddle_high.astype(jnp.float32)).astype(jnp.bfloat16)
    one_hot = (delay_table[:, :, None] == sample_index[None, None, :]).astype(jnp.bfloat16)
    phase_grid = jnp.einsum(
        "cdv,vf->cdf", one_hot, twiddle_high, preferred_element_type=jnp.float32
    ) + jnp.einsum("cdv,vf->cdf", one_hot, twiddle_low, preferred_element_type=jnp.float32)
    cos_grid = phase_grid[:, :, :half]
    sin_grid = phase_grid[:, :, half:]
    highest = lax.Precision.HIGHEST
    series = lax.all_to_all(outgoing, ("section", "sub"), split_axis=1, concat_axis=0, tiled=True)[
        :, 0
    ]
    centred = series - jnp.mean(series, axis=2, keepdims=True)
    spread = jnp.mean(centred * centred, axis=2, keepdims=True)
    normed = centred / jnp.sqrt(spread + 1e-06)
    spec_real = jnp.einsum("cbu,fu->fbc", normed, forward_cos, precision=highest)
    spec_imag = jnp.einsum("cbu,fu->fbc", normed, forward_sin, precision=highest)
    out_real = jnp.einsum("fbc,cdf->fbd", spec_real, cos_grid, precision=highest) - jnp.einsum(
        "fbc,cdf->fbd", spec_imag, sin_grid, precision=highest
    )
    out_imag = jnp.einsum("fbc,cdf->fbd", spec_real, sin_grid, precision=highest) + jnp.einsum(
        "fbc,cdf->fbd", spec_imag, cos_grid, precision=highest
    )
    result = jnp.einsum("fbd,fu->dbu", out_real, inverse_cos, precision=highest) + jnp.einsum(
        "fbd,fu->dbu", out_imag, inverse_sin, precision=highest
    )
    return result / math.sqrt(CHANS)


def solution(mesh):
    return jax.shard_map(
        shards,
        mesh=mesh,
        in_specs=(
            P(("groups", "section", "sub"), None, None),
            P(),
            P(("groups", "section", "sub"), None, None, None),
            P(),
            P(),
            P(),
        ),
        out_specs=P(None, ("groups", "section", "sub"), None),
        check_vma=False,
    )
```

profile of v0, /device:TPU:15, one launch (start us, length us, event | category | flops | bytes accessed | tf_op | source)
XLA Modules:
  0.0 1017.0 jit_solution(13702992276436314519)
XLA Ops:
  0.5 49.9 %reshape.190 = bf16[64,2,515,128]{3,2,1,0:T(8,128)(2,1)} reshape(bf16[64,2,65920]{2,1,0:T(2,128)(2,1)} %param.6) | data formatting | bytes 33751040 | tf_op jit(solution)/shard_map/reshape | solution.py:30
  50.4 7.8 fusion.31
  58.2 10.2 %fusion.30 = bf16[64,512,1024]{2,1,0:T(8,128)(2,1)} fusion(bf16[64,512,1024]{2,1,0:T(8,128)(2,1)} %fusion.31, bf16[64,2,515,128]{3,2,1,0:T(8,128)(2,1)} %reshape.190), kind=kLoop, calls=%fused_computation.41 | loop fusion | bytes 16777216
  68.5 10.2 %fusion.29 = bf16[64,512,1024]{2,1,0:T(8,128)(2,1)} fusion(bf16[64,512,1024]{2,1,0:T(8,128)(2,1)} %fusion.30, bf16[64,2,515,128]{3,2,1,0:T(8,128)(2,1)} %reshape.190), kind=kLoop, calls=%fused_computation.39 | loop fusion | bytes 16777216
  78.7 10.3 %fusion.28 = bf16[64,512,1024]{2,1,0:T(8,128)(2,1)} fusion(bf16[64,512,1024]{2,1,0:T(8,128)(2,1)} %fusion.29, bf16[64,2,515,128]{3,2,1,0:T(8,128)(2,1)} %reshape.190), kind=kLoop, calls=%fused_computation.37 | loop fusion | bytes 16777216
  89.0 7.9 fusion.27
  96.9 10.6 %fusion.26 = bf16[64,512,1024]{2,1,0:T(8,128)(2,1)} fusion(bf16[64,512,1024]{2,1,0:T(8,128)(2,1)} %fusion.27, bf16[64,2,515,128]{3,2,1,0:T(8,128)(2,1)} %reshape.190), kind=kLoop, calls=%fused_computation.33 | loop fusion | bytes 16777216
  107.5 10.2 %fusion.25 = bf16[64,512,1024]{2,1,0:T(8,128)(2,1)} fusion(bf16[64,512,1024]{2,1,0:T(8,128)(2,1)} %fusion.26, bf16[64,2,515,128]{3,2,1,0:T(8,128)(2,1)} %reshape.190), kind=kLoop, calls=%fused_computation.31 | loop fusion | bytes 16777216
  117.7 10.3 %fusion.24 = bf16[64,512,1024]{2,1,0:T(8,128)(2,1)} fusion(bf16[64,512,1024]{2,1,0:T(8,128)(2,1)} %fusion.25, bf16[64,2,515,128]{3,2,1,0:T(8,128)(2,1)} %reshape.190), kind=kLoop, calls=%fused_computation.29 | loop fusion | bytes 16777216 | tf_op jit(solution)/shard_map/concatenate | solution.py:31
  128.2 34.0 %fusion.14 = bf16[2,128,64,512]{3,1,2,0:T(8,128)(2,1)} fusion(bf16[64,512,1024]{2,1,0:T(8,128)(2,1)} %fusion.24, bf16[1,128,1024]{2,1,0:T(8,128)(2,1)S(1)} %get-tuple-element.10, bf16[1,128,1024]{2,1,0:T(8,128)(2,1)S(1)} %get-tuple-element.9), kind=kOutput, calls=%fused_computation.24 | convolution fusion | flops 17189306368 | bytes 84410368 | tf_op jit(solution)/shard_map/dot_general | solution.py:39
  162.3 18.5 %copy.81 = bf16[2,128,64,512]{3,2,0,1:T(8,128)(2,1)} copy(bf16[2,128,64,512]{3,1,2,0:T(8,128)(2,1)} %fusion.14) | data formatting | bytes 33554432 | tf_op jit(solution)/shard_map/convert_element_type | solution.py:42
  197.6 352.0 %all-to-all-done = bf16[2,128,64,512]{3,2,0,1:T(8,128)(2,1)} async-done(((bf16[2,128,64,512]{3,2,0,1:T(8,128)(2,1)}), bf16[2,128,64,512]{3,2,0,1:T(8,128)(2,1)}, u32[]{:S(2)}, u32[]{:S(2)}) %all-to-all-start) | async-done | bytes 16777248 | tf_op jit(solution)/shard_map/all_to_all | solution.py:66
  549.6 8.7 copy.83
  558.3 39.3 %copy.84 = bf16[2,8,1024,512]{3,1,2,0:T(8,128)(2,1)} copy(bf16[2,8,1024,512]{3,2,1,0:T(8,128)(2,1)S(1)} %bitcast.159) | data formatting | bytes 33554432 | tf_op jit(solution)/shard_map/all_to_all | solution.py:66
  597.7 18.2 %gather_fusion.1 = bf16[1024,2,8,512]{3,2,1,0:T(8,128)(2,1)} fusion(bf16[2,8,1024,512]{3,1,2,0:T(8,128)(2,1)} %copy.84, s32[1024]{0:T(1024)S(1)} %fusion.112), kind=kCustom, calls=%fused_computation.1 | custom fusion | bytes 33558528 | tf_op jit(solution)/shard_map/jit(_take)/gather | solution.py:65
  615.9 14.9 %select_bitcast_fusion = bf16[2,8,1024,512]{3,1,0,2:T(8,128)(2,1)} fusion(bf16[1024,2,8,512]{3,2,1,0:T(8,128)(2,1)} %gather_fusion.1, pred[1024]{0:T(1024)(128)(4,1)S(1)} %compare_and_fusion), kind=kLoop, calls=%fused_computation.17 | loop fusion | flops 8388608 | bytes 33555456 | tf_op jit(solution)/shard_map/jit(_take)/select_n | solution.py:65
  630.8 23.2 %copy.86 = bf16[2,8,1024,512]{2,3,0,1:T(8,128)(2,1)} copy(bf16[2,8,1024,512]{3,1,0,2:T(8,128)(2,1)} %select_bitcast_fusion) | data formatting | bytes 33554432 | tf_op jit(solution)/shard_map/jit(_take)/select_n | solution.py:65
  654.0 32.2 %fusion.17 = f32[2,8,1024,512]{2,3,0,1:T(8,128)} fusion(bf16[2,8,1024,512]{2,3,0,1:T(8,128)(2,1)} %copy.86, bf16[8,2,1024,1024]{3,2,1,0:T(8,128)(2,1)} %param.8), kind=kOutput, calls=%fused_computation.25 | convolution fusion | flops 17179869184 | bytes 67108864 | tf_op jit(solution)/shard_map/cbi,pcit->pcbt/dot_general | solution.py:70
  686.2 32.5 %fusion.20 = f32[2,8,1024,512]{2,3,0,1:T(8,128)} fusion(bf16[2,8,1024,512]{2,3,0,1:T(8,128)(2,1)} %copy.86, bf16[8,2,1024,1024]{3,2,1,0:T(8,128)(2,1)} %param.8), kind=kOutput, calls=%fused_computation.26 | convolution fusion | flops 17179869184 | bytes 67108864 | tf_op jit(solution)/shard_map/cbi,pcit->pcbt/dot_general | solution.py:73
  718.7 29.5 %fusion.4 = f32[8,1024,512]{1,2,0:T(8,128)} fusion(f32[2,8,1024,512]{2,3,0,1:T(8,128)} %fusion.20, f32[2,8,1024,512]{2,3,0,1:T(8,128)} %fusion.17), kind=kLoop, calls=%fused_computation.10 | loop fusion | flops 20971520 | bytes 83886080 | tf_op jit(solution)/shard_map/add | solution.py:78
  748.2 17.5 %copy.89 = f32[8,1024,512]{2,0,1:T(8,128)} copy(f32[8,1024,512]{1,2,0:T(8,128)} %fusion.4) | data formatting | bytes 33554432 | tf_op jit(solution)/shard_map/add | solution.py:78
  765.8 18.2 %gather_fusion.2 = f32[1024,8,512]{2,1,0:T(8,128)} fusion(f32[8,1024,512]{2,0,1:T(8,128)} %copy.89, s32[1024]{0:T(1024)S(1)} %fusion.111), kind=kCustom, calls=%fused_computation.2 | custom fusion | bytes 33558528 | tf_op jit(solution)/shard_map/jit(_take)/gather | solution.py:79
  784.0 16.6 %copy.90 = f32[8,1024,512]{1,0,2:T(8,128)} copy(f32[8,1024,512]{2,0,1:T(8,128)} %bitcast.158) | data formatting | bytes 33554432 | tf_op jit(solution)/shard_map/jit(_take)/gather | solution.py:79
  800.6 10.8 %select_reduce_fusion = f32[8,1024,128]{1,0,2:T(8,128)} fusion(pred[1024]{0:T(1024)(128)(4,1)S(1)} %copy-done.5, f32[8,1024,512]{1,0,2:T(8,128)} %copy.90), kind=kLoop, calls=%fused_computation.21 | loop fusion | flops 7340032 | bytes 20972544 | tf_op jit(solution)/shard_map/reduce_sum | solution.py:47
  848.3 70.8 %all-to-all-done.1 = f32[8,16,64,128]{3,2,0,1:T(8,128)} async-done(((f32[8,16,64,128]{3,2,0,1:T(8,128)}), f32[8,16,64,128]{3,2,0,1:T(8,128)}, u32[]{:S(2)}, u32[]{:S(2)}) %all-to-all-start.1) | async-done | bytes 4194336 | tf_op jit(solution)/shard_map/all_to_all | solution.py:114
  946.8 10.2 %fusion.36 = f32[65,64,256]{2,1,0:T(8,128)} fusion(f32[128,256,65]{1,2,0:T(8,128)S(1)} %bitcast.157, f32[65,128,64]{1,0,2:T(8,128)S(1)} %fusion.49), kind=kOutput, calls=%fused_computation.49 | convolution fusion | flops 1635778560 | bytes 14909440 | tf_op jit(solution)/shard_map/fbc,cdf->fbd/dot_general | solution.py:122
  957.0 9.9 fusion.34
  966.9 9.4 fusion.55
  976.2 10.0 fusion.58
  986.2 9.8 fusion.42
  996.0 11.9 %multiply_bitcast_fusion = f32[256,64,128]{0,2,1:T(8,128)} fusion(f32[128,64,256]{2,0,1:T(8,128)S(1)} %fusion.42, f32[65,64,256]{2,1,0:T(8,128)S(1)} %fusion.55, f32[65]{0:T(128)S(1)} %fusion.115), kind=kOutput, calls=%fused_computation.44 | convolution fusion | flops 1640097664 | bytes 21037316 | tf_op jit(solution)/shard_map/fbd,fu->dbu/dot_general | solution.py:128
  1007.9 8.7 copy.111
  (66 shorter events, 81.8 us)
Async XLA Ops:
  0.0 188.1 %copy-start = (s32[1024]{0:T(1024)S(1)}, s32[1024]{0:T(1024)}, u32[]{:S(2)}) copy-start(s32[1024]{0:T(1024)} %param.9) | copy-start | bytes 12292
  117.7 10.4 %copy-start.6 = (f32[512]{0:T(512)S(1)}, f32[512]{0:T(512)}, u32[]{:S(2)}) copy-start(f32[512]{0:T(512)} %param.7) | copy-start | bytes 6148
  180.8 16.2 %copy-start.4 = (s32[1024]{0:T(1024)S(1)}, s32[1024]{0:T(1024)}, u32[]{:S(2)}) copy-start(s32[1024]{0:T(1024)} %param.10) | copy-start | bytes 12292
  180.8 368.8 %all-to-all-start = ((bf16[2,128,64,512]{3,2,0,1:T(8,128)(2,1)}), bf16[2,128,64,512]{3,2,0,1:T(8,128)(2,1)}, u32[]{:S(2)}, u32[]{:S(2)}) async-start(bf16[2,128,64,512]{3,2,0,1:T(8,128)(2,1)} %copy.81), calls=%async_computation | async-start | bytes 33554432 | tf_op jit(solution)/shard_map/all_to_all | solution.py:66
  784.0 16.6 %copy-start.5 = (pred[1024]{0:T(1024)(128)(4,1)S(1)}, pred[1024]{0:T(1024)(128)(4,1)}, u32[]{:S(2)}) copy-start(pred[1024]{0:T(1024)(128)(4,1)} %compare_and_fusion.1) | copy-start | bytes 3076
  816.8 10.1 copy-start.3
  821.6 97.6 %all-to-all-start.1 = ((f32[8,16,64,128]{3,2,0,1:T(8,128)}), f32[8,16,64,128]{3,2,0,1:T(8,128)}, u32[]{:S(2)}, u32[]{:S(2)}) async-start(f32[8,16,64,128]{3,2,0,1:T(8,128)} %copy.92), calls=%async_computation.1 | async-start | bytes 8388608 | tf_op jit(solution)/shard_map/all_to_all | solution.py:114
  926.6 20.1 %slice-start.3 = ((s8[9437184]{0:T(1024)(128)(4,1)}), s8[4194304]{0:T(1024)(128)(4,1)S(1)}, s32[]{:S(2)}) async-start(s8[9437184]{0:T(1024)(128)(4,1)} %bitcast.156), calls=%async_computation.5 | async-start | bytes 8388608
  926.6 20.1 %slice-start.4 = ((s8[9437184]{0:T(1024)(128)(4,1)}), s8[4194304]{0:T(1024)(128)(4,1)S(1)}, s32[]{:S(2)}) async-start(s8[9437184]{0:T(1024)(128)(4,1)} %bitcast.156), calls=%async_computation.6 | async-start | bytes 8388608
  933.4 13.4 %slice-start.5 = ((s8[9437184]{0:T(1024)(128)(4,1)}), s8[1048576]{0:T(1024)(128)(4,1)S(1)}, s32[]{:S(2)}) async-start(s8[9437184]{0:T(1024)(128)(4,1)} %bitcast.156), calls=%async_computation.7 | async-start | bytes 2097152
  946.7 20.1 %copy-start.2 = (f32[65,128,64]{1,0,2:T(8,128)}, f32[65,128,64]{1,0,2:T(8,128)S(1)}, u32[]{:S(2)}) copy-start(f32[65,128,64]{1,0,2:T(8,128)S(1)} %fusion.51) | copy-start | bytes 6389764
  946.8 20.1 %slice-start = ((s8[9437184]{0:T(1024)(128)(4,1)}), s8[4194304]{0:T(1024)(128)(4,1)S(1)}, s32[]{:S(2)}) async-start(s8[9437184]{0:T(1024)(128)(4,1)} %bitcast.154), calls=%async_computation.2 | async-start | bytes 8388608
  946.8 20.1 %slice-start.1 = ((s8[9437184]{0:T(1024)(128)(4,1)}), s8[4194304]{0:T(1024)(128)(4,1)S(1)}, s32[]{:S(2)}) async-start(s8[9437184]{0:T(1024)(128)(4,1)} %bitcast.154), calls=%async_computation.3 | async-start | bytes 8388608
  957.0 9.9 slice-start.2
  996.0 20.6 %copy-start.1 = (s32[1024]{0:T(1024)S(1)}, s32[1024]{0:T(1024)}, u32[]{:S(2)}) copy-start(s32[1024]{0:T(1024)} %param.9) | copy-start | bytes 12292
where the time goes:
time: 1030 us; the launch traced here: 1020 us
  waiting for transfers between devices  423 us (41%)
  local copies, waits for them, and re-layouts  324 us (31%)
  matrix products  186 us (18%)
  other arithmetic  71.4 us (7%)
  starting transfers between devices  11.9 us (1%)
    all_to_all x1, waiting for transfers between devices, shards(): lax.all_to_all(spectra_local, ('section', 'sub'), split_axis=1, concat_ax...  352 us
    all_to_all x1, waiting for transfers between devices, shards(): lax.all_to_all(outgoing, ('section', 'sub'), split_axis=1, concat_axis=0,...  70.8 us
    unnamed x34, local copies, waits for them, and re-layouts  67.5 us
    reshape x1, local copies, waits for them, and re-layouts, channelize(): frames = block_volts.reshape(input_count, 2, SPECTRA + TAPS - 1, CHANS)  49.9 us
    all_to_all x2, local copies, waits for them, and re-layouts, shards(): lax.all_to_all(spectra_local, ('section', 'sub'), split_axis=1, concat_ax...  48.1 us
    gather x2, local copies, waits for them, and re-layouts, shards(): power = jnp.take(power, beam_order, axis=1)  34.9 us
    dot_general x1, matrix products, channelize(): lax.dot_general(matrix, windows, (((2,), (2,)), ((), ())), preferred_elem...  34 us
    dot_general x1, matrix products, shards(): jnp.einsum('cbi,pcit->pcbt', weight_imag, ordered, preferred_element_type...  32.5 us
  transfers between devices with their start and end apart: 2, of which 2 were waited for; matrix products, arithmetic and copies ran while one was open for 3% of the time, Pallas kernels for 0%

commit v1 on v0

v1 whole, which is shorter than its diff:
```python
import functools
import math

import jax
import jax.numpy as jnp
import numpy as np
from jax import lax
from jax.experimental import pallas as pl
from jax.experimental.pallas import tpu as pltpu
from jax.sharding import PartitionSpec as P

CHANS = 128
INPUTS = 1024
BEAMS = 1024
TAPS = 4
DOWN = 4
SPECTRA = 512
BINS = 128
SLOTS = 8
MESH = pl.DeviceIdType.MESH
NT = (((1,), (1,)), ((), ()))
NN = (((1,), (0,)), ((), ()))


def filter_matrix(prototype):
    channel_index = np.arange(CHANS)
    phase_step = channel_index[:, None] * channel_index[None, :] % CHANS
    angles = 2.0 * math.pi / CHANS * phase_step
    cosine = np.tile(np.cos(angles), (1, TAPS))
    sine = np.tile(np.sin(angles), (1, TAPS))
    table = np.concatenate(
        [np.concatenate([cosine, sine], axis=1), np.concatenate([-sine, cosine], axis=1)], axis=0
    ).astype(np.float32)
    return (table * jnp.tile(prototype, 2)[None, :]).astype(jnp.bfloat16)


def dot(a, b, dims=NN):
    return lax.dot_general(a, b, dims, preferred_element_type=jnp.float32)


def exchange_kernel(
    owners,
    subs,
    frames_ref,
    filter_ref,
    weights_ref,
    pick_ref,
    beams_ref,
    series_ref,
    landing_ref,
    frame_buf,
    wide,
    stage,
    outbox,
    weight_buf,
    steered,
    spectra,
    normed,
    power,
    frame_sem,
    weight_sem,
    own_sem,
    load_sem,
    early_send_sem,
    early_recv_sem,
    send_sem,
    recv_sem,
    power_own_sem,
    power_send_sem,
    power_recv_sem,
):
    inputs = frames_ref.shape[0]
    chan_dev = weights_ref.shape[0]
    group = min(16, inputs)
    blocks = inputs // group
    me = lax.axis_index("section") * subs + lax.axis_index("sub")

    def place(owner):
        return {"section": owner // subs, "sub": owner % subs}

    def partner(step):
        return (me + step) % owners

    barrier = pltpu.get_barrier_semaphore()

    def greet(step, carry):
        pl.semaphore_signal(
            barrier, inc=1, device_id=place((me + step) % owners), device_id_type=MESH
        )
        return carry

    lax.fori_loop(1, owners, greet, 0)

    def frame_copy(index):
        slot = index % SLOTS
        return pltpu.make_async_copy(
            frames_ref.at[index], frame_buf.at[slot], frame_sem.at[slot]
        )

    def weight_copy(chan):
        slot = chan % 2
        return pltpu.make_async_copy(
            weights_ref.at[chan], weight_buf.at[slot], weight_sem.at[slot]
        )

    def spectra_copy(chan, owner, source):
        return pltpu.make_async_remote_copy(
            src_ref=outbox.at[owner * chan_dev + chan],
            dst_ref=landing_ref.at[chan, source],
            send_sem=send_sem.at[chan, owner],
            recv_sem=recv_sem.at[chan, source],
            device_id=place(owner),
            device_id_type=MESH,
        )

    def early_copy(block, owner, source):
        rows = pl.ds(pl.multiple_of(block * 2 * group, 2 * group), 2 * group)
        return pltpu.make_async_remote_copy(
            src_ref=outbox.at[owner * chan_dev, rows],
            dst_ref=landing_ref.at[0, source, rows],
            send_sem=early_send_sem.at[block, owner],
            recv_sem=early_recv_sem.at[block, source],
            device_id=place(owner),
            device_id_type=MESH,
        )

    def own_copy(chan):
        return pltpu.make_async_copy(
            outbox.at[me * chan_dev + chan], landing_ref.at[chan, me], own_sem.at[chan]
        )

    def power_copy(chan, owner, source):
        return pltpu.make_async_remote_copy(
            src_ref=power.at[chan, owner],
            dst_ref=series_ref.at[source * chan_dev + chan],
            send_sem=power_send_sem.at[chan, owner],
            recv_sem=power_recv_sem.at[chan, source],
            device_id=place(owner),
            device_id_type=MESH,
        )

    def power_own_copy(chan):
        return pltpu.make_async_copy(
            power.at[chan, me], series_ref.at[me * chan_dev + chan], power_own_sem.at[chan]
        )

    for index in range(min(SLOTS - 1, inputs)):
        frame_copy(index).start()
    weight_copy(0).start()

    def channelize(index, slot, member):
        edges = []
        for part in range(2):
            wide[part] = frame_buf[slot, part].astype(jnp.float32)
            edges.append(
                [
                    wide[part, pl.ds(s, BINS, stride=DOWN), :].astype(jnp.bfloat16)
                    for s in range(DOWN + TAPS - 1)
                ]
            )
        for m in range(DOWN):
            window = jnp.concatenate(edges[0][m : m + TAPS] + edges[1][m : m + TAPS], axis=1)
            stage[m, pl.ds(member, 2 * CHANS, stride=group), :] = dot(
                filter_ref[...], window, NT
            )

    def input_group(block, carry):
        def one(member, inner):
            index = block * group + member
            frame_copy(index).wait()

            @pl.when(index + SLOTS - 1 < inputs)
            def _():
                frame_copy(index + SLOTS - 1).start()

            channelize(index, index % SLOTS, member)
            return inner

        lax.fori_loop(0, group, one, 0)

        def spread(chan, inner):
            halves = []
            for p in range(2):
                at_row = pl.ds(pl.multiple_of((p * CHANS + chan) * group, group), group)
                halves.append(
                    jnp.concatenate([stage[m, at_row, :] for m in range(DOWN)], axis=1)
                )
            row = pl.multiple_of(block * 2 * group, 2 * group)
            outbox[chan, pl.ds(row, 2 * group), :] = jnp.concatenate(halves, axis=0).astype(
                jnp.bfloat16
            )
            return inner

        lax.fori_loop(0, CHANS, spread, 0, unroll=4)

        def send_early(step, inner):
            early_copy(block, partner(step), me).start()
            return inner

        lax.fori_loop(1, owners, send_early, 0)
        return carry

    pl.semaphore_wait(barrier, owners - 1)
    lax.fori_loop(0, blocks, input_group, 0)
    own_copy(0).start()

    def send_channel(chan, carry):
        own_copy(chan).start()

        def send(step, inner):
            spectra_copy(chan, partner(step), me).start()
            return inner

        lax.fori_loop(1, owners, send, 0)
        return carry

    lax.fori_loop(1, chan_dev, send_channel, 0)

    columns = 512
    rows = 256
    lane = lax.broadcasted_iota(jnp.int32, (rows, columns), 1)

    def one_channel(chan, carry):
        slot = chan % 2
        weight_copy(chan).wait()

        @pl.when(chan + 1 < chan_dev)
        def _():
            weight_copy(chan + 1).start()

        def steer_rows(tile, inner):
            at_row = pl.ds(pl.multiple_of(tile * rows, rows), rows)
            real = weight_buf[slot, 0, at_row, :]
            imag = weight_buf[slot, 1, at_row, :]
            for start in range(0, 2 * INPUTS, columns):
                pick = pick_ref[:, start : start + columns]
                picked_real = dot(real, pick)
                picked_imag = dot(imag, pick)
                first = ((lane + start) // group) % 2 == 0
                steered[0, at_row, start : start + columns] = jnp.where(
                    first, picked_real, -picked_imag
                ).astype(jnp.bfloat16)
                steered[1, at_row, start : start + columns] = jnp.where(
                    first, picked_imag, picked_real
                ).astype(jnp.bfloat16)
            return inner

        lax.fori_loop(0, BEAMS // rows, steer_rows, 0)

        own_copy(chan).wait()

        def arrive(step, inner):
            source = (me + step) % owners

            @pl.when(chan == 0)
            def _():
                for block in range(blocks):
                    early_copy(block, source, source).wait_recv()

            @pl.when(chan > 0)
            def _():
                spectra_copy(chan, source, source).wait_recv()

            return inner

        lax.fori_loop(1, owners, arrive, 0)
        load = pltpu.make_async_copy(landing_ref.at[chan], spectra, load_sem)
        load.start()
        load.wait()

        def form_rows(tile, inner):
            at_row = pl.ds(pl.multiple_of(tile * rows, rows), rows)
            field = spectra[...].reshape(2 * INPUTS, SPECTRA)
            real = dot(steered[0, at_row, :], field)
            imag = dot(steered[1, at_row, :], field)
            squares = real * real + imag * imag
            folded = squares[:, 0:BINS]
            for m in range(1, DOWN):
                folded = folded + squares[:, m * BINS : (m + 1) * BINS]
            centred = folded - jnp.mean(folded, axis=1, keepdims=True)
            spread = jnp.mean(centred * centred, axis=1, keepdims=True)
            normed[at_row, :] = (centred / jnp.sqrt(spread + 1e-06)).astype(jnp.bfloat16)
            return inner

        lax.fori_loop(0, BEAMS // rows, form_rows, 0)
        stored = dot(beams_ref[...], normed[...])
        power[chan] = stored.reshape(power.shape[1:]).astype(jnp.bfloat16)
        power_own_copy(chan).start()

        def send(step, inner):
            power_copy(chan, partner(step), me).start()
            return inner

        lax.fori_loop(1, owners, send, 0)
        return carry

    lax.fori_loop(0, chan_dev, one_channel, 0)

    def finish(chan, carry):
        power_own_copy(chan).wait()

        def drain(step, inner):
            other = (me + step) % owners

            @pl.when(chan == 0)
            def _():
                for block in range(blocks):
                    early_copy(block, other, me).wait_send()

            @pl.when(chan > 0)
            def _():
                spectra_copy(chan, other, me).wait_send()

            power_copy(chan, other, me).wait_send()
            power_copy(chan, other, other).wait_recv()
            return inner

        lax.fori_loop(1, owners, drain, 0)
        return carry

    lax.fori_loop(0, chan_dev, finish, 0)


def exchange(frames, matrix, beam_weights, pick, beams, owners, subs):
    inputs = frames.shape[0]
    chan_dev = beam_weights.shape[0]
    beam_dev = BEAMS // owners
    group = min(16, inputs)
    any_space = pl.BlockSpec(memory_space=pl.ANY)
    vmem = pl.BlockSpec(memory_space=pltpu.VMEM)
    series, _ = pl.pallas_call(
        functools.partial(exchange_kernel, owners, subs),
        out_shape=(
            jax.ShapeDtypeStruct((CHANS, beam_dev, BINS), jnp.bfloat16),
            jax.ShapeDtypeStruct((chan_dev, owners, 2 * inputs, SPECTRA), jnp.bfloat16),
        ),
        in_specs=[any_space, vmem, any_space, vmem, vmem],
        out_specs=(any_space, any_space),
        scratch_shapes=[
            pltpu.VMEM((SLOTS,) + frames.shape[1:], jnp.bfloat16),
            pltpu.VMEM(frames.shape[1:], jnp.float32),
            pltpu.VMEM((DOWN, 2 * CHANS * group, BINS), jnp.float32),
            pltpu.VMEM((CHANS, 2 * inputs, SPECTRA), jnp.bfloat16),
            pltpu.VMEM((2, 2, BEAMS, INPUTS), jnp.bfloat16),
            pltpu.VMEM((2, BEAMS, 2 * INPUTS), jnp.bfloat16),
            pltpu.VMEM((owners, 2 * inputs, SPECTRA), jnp.bfloat16),
            pltpu.VMEM((BEAMS, BINS), jnp.bfloat16),
            pltpu.VMEM((chan_dev, owners, beam_dev, BINS), jnp.bfloat16),
            pltpu.SemaphoreType.DMA((SLOTS,)),
            pltpu.SemaphoreType.DMA((2,)),
            pltpu.SemaphoreType.DMA((chan_dev,)),
            pltpu.SemaphoreType.DMA,
            pltpu.SemaphoreType.DMA((inputs // group, owners)),
            pltpu.SemaphoreType.DMA((inputs // group, owners)),
            pltpu.SemaphoreType.DMA((chan_dev, owners)),
            pltpu.SemaphoreType.DMA((chan_dev, owners)),
            pltpu.SemaphoreType.DMA((chan_dev,)),
            pltpu.SemaphoreType.DMA((chan_dev, owners)),
            pltpu.SemaphoreType.DMA((chan_dev, owners)),
        ],
        compiler_params=pltpu.CompilerParams(
            collective_id=0, has_side_effects=True, vmem_limit_bytes=60 * 1024 * 1024
        ),
        name="exchange",
    )(frames, matrix, beam_weights, pick, beams)
    return series


def split_pair(array):
    high = array.astype(jnp.bfloat16)
    low = (array - high.astype(np.float64)).astype(jnp.bfloat16)
    return high, low


def dedisperse_kernel(
    series_ref, turn_ref, forward_ref, inverse_ref, out_ref, spectrum, turned, phase
):
    beams = series_ref.shape[1]
    trials = turn_ref.shape[1]
    half = BINS // 2 + 1
    joined = BINS // beams
    chan_rows = CHANS // joined
    trial_rows = trials // joined

    def transform(row, carry):
        block = jnp.concatenate(
            [series_ref[r * chan_rows + row].astype(jnp.float32) for r in range(joined)], axis=0
        ).astype(jnp.bfloat16)
        spectrum[pl.ds(row, BINS, stride=chan_rows), :] = dot(
            forward_ref[0], block, NT
        ) + dot(forward_ref[1], block, NT)
        return carry

    lax.fori_loop(0, chan_rows, transform, 0, unroll=4)

    def slab(index):
        rows = spectrum[pl.ds(pl.multiple_of(index * chan_rows, chan_rows), chan_rows), :]
        return jnp.concatenate(
            [rows[:, r * beams : (r + 1) * beams] for r in range(joined)], axis=0
        ).astype(jnp.bfloat16)

    def put(index, value):
        turned[pl.ds(pl.multiple_of(index * trial_rows, trial_rows), trial_rows), :] = (
            jnp.concatenate(
                [value[r * trial_rows : (r + 1) * trial_rows] for r in range(joined)], axis=1
            )
        )

    ones = jnp.ones((trials, CHANS), jnp.bfloat16)
    put(0, dot(ones, slab(0)))
    phase[...] = turn_ref[...]

    def rotate(freq, carry):
        cos_now = phase[0]
        sin_now = phase[1]
        cos_half = cos_now.astype(jnp.bfloat16)
        sin_half = sin_now.astype(jnp.bfloat16)
        both = jnp.concatenate([slab(freq), slab(freq + half - 1)], axis=0)
        put(freq, dot(jnp.concatenate([cos_half, -sin_half], axis=1), both))
        put(freq + half - 1, dot(jnp.concatenate([sin_half, cos_half], axis=1), both))
        phase[0] = cos_now * turn_ref[0] - sin_now * turn_ref[1]
        phase[1] = cos_now * turn_ref[1] + sin_now * turn_ref[0]
        return carry

    lax.fori_loop(1, half - 1, rotate, 0)
    put(half - 1, dot(phase[0].astype(jnp.bfloat16), slab(half - 1)))

    def restore(row, carry):
        rows = turned[pl.ds(row, BINS, stride=trial_rows), :].astype(jnp.bfloat16)
        rows = jnp.concatenate([rows, rows], axis=0)
        result = dot(rows, inverse_ref[...], (((0,), (0,)), ((), ())))
        for r in range(joined):
            out_ref[r * trial_rows + row] = result[r * beams : (r + 1) * beams]
        return carry

    lax.fori_loop(0, trial_rows, restore, 0, unroll=4)


def dedisperse(series, trial_delays):
    half = BINS // 2 + 1
    beams = series.shape[1]
    trials = trial_delays.shape[0]
    sample_index = np.arange(BINS)
    freq_index = np.arange(half)
    angles = 2.0 * math.pi / BINS * (freq_index[:, None] * sample_index[None, :] % BINS)
    forward = np.concatenate([np.cos(angles), -np.sin(angles)[1 : half - 1]], axis=0)
    edge = (freq_index == 0) | (freq_index == BINS // 2)
    fold_weight = np.where(edge, 1.0, 2.0) / BINS / math.sqrt(CHANS)
    inverse = np.concatenate([fold_weight, fold_weight[1 : half - 1]])[:, None] * forward
    turn_angle = 2.0 * math.pi / BINS * trial_delays.astype(jnp.float32)
    turn = jnp.stack([jnp.cos(turn_angle), jnp.sin(turn_angle)])
    vmem = pl.BlockSpec(memory_space=pltpu.VMEM)
    return pl.pallas_call(
        dedisperse_kernel,
        out_shape=jax.ShapeDtypeStruct((trials, beams, BINS), jnp.float32),
        in_specs=[vmem] * 4,
        out_specs=vmem,
        scratch_shapes=[
            pltpu.VMEM((BINS * CHANS * beams // BINS, BINS), jnp.float32),
            pltpu.VMEM((BINS * trials * beams // BINS, BINS), jnp.float32),
            pltpu.VMEM((2, trials, CHANS), jnp.float32),
        ],
        compiler_params=pltpu.CompilerParams(vmem_limit_bytes=56 * 1024 * 1024),
        name="dedisperse",
    )(
        series,
        turn,
        np.stack(split_pair(forward)),
        np.concatenate(split_pair(inverse), axis=0),
    )


def shards(voltages, prototype, beam_weights, input_order, beam_order, trial_delays):
    subs = lax.axis_size("sub")
    owners = lax.axis_size("section") * subs
    inputs = voltages.shape[0]
    frames = voltages.reshape(inputs, 2, SPECTRA + TAPS - 1, CHANS)
    physical = jnp.arange(INPUTS, dtype=jnp.int32)
    group = min(16, inputs)
    by_block = jnp.broadcast_to(
        input_order.reshape(INPUTS // group, 1, group), (INPUTS // group, 2, group)
    ).reshape(2 * INPUTS)
    pick = (physical[:, None] == by_block[None, :]).astype(jnp.bfloat16)
    beams = (beam_order[:, None] == physical[None, :]).astype(jnp.bfloat16)
    series = exchange(
        frames, filter_matrix(prototype), beam_weights, pick, beams, owners, subs
    )
    return dedisperse(series, trial_delays)


def solution(mesh):
    return jax.shard_map(
        shards,
        mesh=mesh,
        in_specs=(
            P(("groups", "section", "sub"), None, None),
            P(),
            P(("groups", "section", "sub"), None, None, None),
            P(),
            P(),
            P(),
        ),
        out_specs=P(None, ("groups", "section", "sub"), None),
        check_vma=False,
    )
```

time: 1030 us -> 550 us (0.53); the launches traced: 1020 us -> 548 us
  Pallas kernels: 0 us -> 490 us
  waiting for transfers between devices: 423 us -> 0 us
  local copies, waits for them, and re-layouts: 324 us -> 50.2 us
  matrix products: 186 us -> 0 us
  other arithmetic: 71.4 us -> 7.67 us
  starting transfers between devices: 11.9 us -> 0 us
    pallas_call x0 -> x2, Pallas kernels: none -> 490 us  [the longest x1 445 us: exchange(): pl.pallas_call(functools.partial(exchange_kernel, owners, subs), out_shap...]
    all_to_all x2 -> x0, waiting for transfers between devices: 423 us -> none  [the longest x1 352 us: shards(): lax.all_to_all(spectra_local, ('section', 'sub'), split_axis=1, concat_ax...]
    dot_general x13 -> x0, matrix products: 186 us -> none  [the longest x1 34 us: channelize(): lax.dot_general(matrix, windows, (((2,), (2,)), ((), ())), preferred_elem...]
    unnamed x34 -> x14, local copies, waits for them, and re-layouts: 67.5 us -> 0.03 us
    gather x5 -> x0, local copies, waits for them, and re-layouts: 58.5 us -> none  [the longest x2 34.9 us: shards(): power = jnp.take(power, beam_order, axis=1)]
    all_to_all x2 -> x0, local copies, waits for them, and re-layouts: 48.1 us -> none  [shards(): lax.all_to_all(spectra_local, ('section', 'sub'), split_axis=1, concat_ax...]
    add x1 -> x0, other arithmetic: 29.5 us -> none  [shards(): power = beam_real * beam_real + beam_imag * beam_imag]
    select_n x1 -> x0, local copies, waits for them, and re-layouts: 23.2 us -> none  [shards(): jnp.take(lax.all_to_all(spectra_local, ('section', 'sub'), split_axis=1,...]
  transfers between devices with their start and end apart: 2 -> 0, of which waited for: 2 -> 0; matrix products, arithmetic and copies ran while one was open for 3% -> 0% of each run, Pallas kernels for 0% -> 0%
where the time goes in v1:
time: 550 us; the launch traced here: 548 us
  Pallas kernels  490 us (89%)
  local copies, waits for them, and re-layouts  50.2 us (9%)
  other arithmetic  7.67 us (1%)
    pallas_call x1, Pallas kernels, exchange(): pl.pallas_call(functools.partial(exchange_kernel, owners, subs), out_shap...  445 us
    reshape x1, local copies, waits for them, and re-layouts, shards(): frames = voltages.reshape(inputs, 2, SPECTRA + TAPS - 1, CHANS)  50 us
    pallas_call x1, Pallas kernels, dedisperse(): pl.pallas_call(dedisperse_kernel, out_shape=jax.ShapeDtypeStruct((trials,...  44.5 us

profile of v1, /device:TPU:15, one launch (start us, length us, event | category | flops | bytes accessed | tf_op | source)
XLA Modules:
  0.0 547.8 jit_solution(12151636498572695861)
XLA Ops:
  0.0 0.0 copy-start
  0.0 0.0 copy-start.2
  0.0 0.0 copy-start.5
  0.0 50.0 %reshape.10.frames_ref = bf16[64,2,515,128]{3,2,1,0:T(8,128)(2,1)} reshape(bf16[64,2,65920]{2,1,0:T(2,128)(2,1)} %param.9) | data formatting | bytes 33751040 | tf_op jit(solution)/shard_map/reshape | solution.py:477
  50.0 0.0 copy-done
  50.0 0.0 copy-start.4
  50.0 0.0 copy-done.2
  50.0 0.9 multiply_convert_fusion.filter_ref
  50.9 0.0 copy-done.5
  50.9 0.1 broadcast_in_dim.4
  51.0 0.1 eq.29
  51.1 3.8 fusion.pick_ref
  54.9 0.0 copy-done.4
  54.9 1.8 fusion.1.beams_ref
  56.7 0.0 copy-start.3
  56.7 445.3 %exchange.1 = (bf16[128,64,128]{2,1,0:T(8,128)(2,1)}, bf16[8,16,128,512]{3,2,1,0:T(8,128)(2,1)}) custom-call(bf16[64,2,515,128]{3,2,1,0:T(8,128)(2,1)} %reshape.10.frames_ref, bf16[256,1024]{1,0:T(8,128)(2,1)} %multiply_convert_fusion.filter_ref, bf16[8,2,1024,1024]{3,2,1,0:T(8,128)(2,1)} %weights_ref.1, bf16[1024,2048]{1,0:T(8,128)(2,1)} %fusion.pick_ref, ...), custom_call_target="tpu_custom_call" | custom-call | tf_op jit(solution)/shard_map/exchange/pallas_call | solution.py:331
  502.1 0.0 copy-done.3
  502.1 0.5 cosine_bitcast_fusion
  502.6 0.0 copy-start.1
  502.6 0.7 pad_maximum_fusion.turn_ref
  503.3 44.5 %dedisperse.1 = f32[256,64,128]{2,1,0:T(8,128)} custom-call(bf16[128,64,128]{2,1,0:T(8,128)(2,1)} %get-tuple-element.6.series_ref, f32[2,256,128]{2,1,0:T(8,128)} %pad_maximum_fusion.turn_ref, bf16[2,128,128]{2,1,0:T(8,128)(2,1)} %constant.9.clone.forward_ref, bf16[256,128]{1,0:T(8,128)(2,1)} %constant.10.clone.inverse_ref), custom_call_target="tpu_custom_call" | custom-call | tf_op jit(solution)/shard_map/dedisperse/pallas_call | solution.py:453
  547.8 0.0 copy-done.1
  (3 shorter events, 0.0 us)
Async XLA Ops:
  0.0 50.0 %copy-start = (f32[512]{0:T(512)S(1)}, f32[512]{0:T(512)}, u32[]{:S(2)}) copy-start(f32[512]{0:T(512)} %param.10) | copy-start | bytes 6148
  0.0 50.0 %copy-start.2 = (f32[256,1024]{1,0:T(8,128)S(1)}, f32[256,1024]{1,0:T(8,128)}, u32[]{:S(2)}) copy-start(f32[256,1024]{1,0:T(8,128)} %constant.8.clone) | copy-start | bytes 3145732
  0.0 50.9 %copy-start.5 = (s32[1024]{0:T(1024)S(1)}, s32[1024]{0:T(1024)}, u32[]{:S(2)}) copy-start(s32[1024]{0:T(1024)} %param.12) | copy-start | bytes 12292
  50.0 4.9 copy-start.4
  56.7 445.3 %copy-start.3 = (s32[256,128]{1,0:T(8,128)S(1)}, s32[256,128]{1,0:T(8,128)}, u32[]{:S(2)}) copy-start(s32[256,128]{1,0:T(8,128)} %param.14) | copy-start | bytes 393220
  502.6 45.3 %copy-start.1 = (f32[512]{0:T(512)S(1)}, f32[512]{0:T(512)}, u32[]{:S(2)}) copy-start(f32[512]{0:T(512)} %param.10) | copy-start | bytes 6148
